TPU v7x, 256 devices: a whole 4x4x8 slice. The times are simulated.
256 devices in a mesh: dp: 16 (over y, x), expert: 16 (over z, core).
Axes of the slice: x: 4, y: 4, z: 8, core: 2. Of those that a mesh axis runs over, the one named last changes fastest.
Arguments:
- out_grad: bfloat16 [32768, 3584], P(('dp', 'expert')), may hold values from -1.5 to 1.5
- route_ids: int32 [32768, 2], P(('dp', 'expert')), may hold values from 0 to 15, all different within a row; in each aligned block of 128 rows (0 to 127, 128 to 255, ...) at most 24 rows name the same one
- route_weights: bfloat16 [32768, 2], P(('dp', 'expert')), may hold values from 0.099609375 to 1
- saved_gate_up: bfloat16 [256, 384, 2048], P(('dp', 'expert')), may hold values from -6 to 6
- down_weight: bfloat16 [16, 1024, 3584], P('expert'), may hold values from -0.1875 to 0.1875
Outputs:
- grad_gate_up: bfloat16 [256, 384, 2048], P(('dp', 'expert'))
- grad_weight: bfloat16 [16, 1024, 3584], P('expert', 'dp')
- weight_scales: float32 [16, 32, 3584], P('expert', 'dp')
- grad_route: float32 [32768, 2], P(('dp', 'expert'))
Inputs may be any that keep to these rules, and one draw needn't show every extreme that they name: `route_ids`: each token names 2 different experts. Within the 128 tokens of one device no expert is named by more than 24 tokens, and in every draw some device's block names some expert exactly 24 times.
All inputs are finite; a program needn't handle non-finite values.
Results may differ from a plain program's by a relative error of at most 0.02.
Values may be sent and summed in bfloat16 or wider, within the bound.
A program may use at most 128 MiB of HBM per device.

v0:
```python
import jax
import jax.numpy as jnp
from jax import lax
from jax.sharding import PartitionSpec as P

tiny_scale = 1e-06


def shards(out_grad, route_ids, route_weights, saved_gate_up, down_weight):
    token_count = out_grad.shape[0]
    pick_width = route_ids.shape[1]
    pick_count = token_count * pick_width
    model_width = out_grad.shape[1]
    hidden = down_weight.shape[1]
    experts = lax.axis_size("expert")
    slot_count = saved_gate_up.shape[1]
    capacity = slot_count // experts
    flat_ids = route_ids.reshape(pick_count)
    onehot = (flat_ids[:, None] == jnp.arange(experts, dtype=jnp.int32)[None, :]).astype(jnp.int32)
    slot_rank = jnp.sum((jnp.cumsum(onehot, axis=0) - 1) * onehot, axis=1)
    slot_index = flat_ids * capacity + slot_rank
    token_of = jnp.arange(pick_count, dtype=jnp.int32) // pick_width
    send_rows = (
        jnp.zeros((slot_count, model_width), jnp.bfloat16).at[slot_index].set(out_grad[token_of])
    )
    send_weights = (
        jnp.zeros((slot_count,), jnp.bfloat16).at[slot_index].set(route_weights.reshape(pick_count))
    )
    recv_rows, recv_weights = (
        lax.all_to_all(
            send_rows.reshape(experts, capacity, model_width),
            "expert",
            split_axis=0,
            concat_axis=0,
            tiled=True,
        ),
        lax.all_to_all(
            send_weights.reshape(experts, capacity),
            "expert",
            split_axis=0,
            concat_axis=0,
            tiled=True,
        ),
    )
    grad_rows = recv_rows.reshape(slot_count, model_width)
    row_weights = recv_weights.reshape(slot_count).astype(jnp.float32)
    weight_mat = down_weight[0]
    saved = saved_gate_up[0]
    weighted = (row_weights[:, None] * grad_rows.astype(jnp.float32)).astype(jnp.bfloat16)
    gate_pre = saved[:, :hidden].astype(jnp.float32)
    up_pre = saved[:, hidden:].astype(jnp.float32)
    sigmoid_gate = jax.nn.sigmoid(gate_pre)
    hidden_act = (gate_pre * sigmoid_gate * up_pre).astype(jnp.bfloat16)
    expert_out = jnp.dot(hidden_act, weight_mat, preferred_element_type=jnp.float32)
    route_part = jnp.sum(grad_rows.astype(jnp.float32) * expert_out, axis=1)
    grad_act = lax.dot_general(
        weighted, weight_mat, (((1,), (1,)), ((), ())), preferred_element_type=jnp.float32
    )
    grad_gate = grad_act * up_pre * sigmoid_gate * (1.0 + gate_pre * (1.0 - sigmoid_gate))
    grad_up = grad_act * gate_pre * sigmoid_gate
    grad_pair = jnp.concatenate([grad_gate, grad_up], axis=1).astype(jnp.bfloat16)
    returned = lax.all_to_all(
        route_part.reshape(experts, capacity), "expert", split_axis=0, concat_axis=0, tiled=True
    )
    grad_route = returned.reshape(slot_count)[slot_index].reshape(token_count, pick_width)
    grad_pair, grad_route = (grad_pair, grad_route)
    partial_value = lax.dot_general(
        hidden_act, weighted, (((0,), (0,)), ((), ())), preferred_element_type=jnp.float32
    )
    block_max = jnp.max(jnp.abs(partial_value).reshape(hidden // 32, 32, model_width), axis=1)
    scales = lax.pmax(block_max.astype(jnp.bfloat16), "dp").astype(block_max.dtype) + tiny_scale
    partial_value, scales = (partial_value, scales)
    scaled_terms = (partial_value / jnp.repeat(scales, 32, axis=0)).astype(jnp.bfloat16)
    summed = lax.psum_scatter(scaled_terms, "dp", scatter_dimension=0, tiled=True).astype(
        jnp.float32
    )
    grad_weight = summed.astype(jnp.bfloat16)[None]
    block_share = hidden // 32 // lax.axis_size("dp")
    scale_share = lax.dynamic_slice_in_dim(
        scales, lax.axis_index("dp") * block_share, block_share, 0
    )[None]
    return (grad_pair[None], grad_weight, scale_share, grad_route)


def solution(mesh):
    in_specs = (
        P(("dp", "expert"), None),
        P(("dp", "expert"), None),
        P(("dp", "expert"), None),
        P(("dp", "expert"), None, None),
        P("expert", None, None),
    )
    out_specs = (
        P(("dp", "expert"), None, None),
        P("expert", "dp", None),
        P("expert", "dp", None),
        P(("dp", "expert"), None),
    )
    return jax.shard_map(shards, mesh=mesh, in_specs=in_specs, out_specs=out_specs, check_vma=False)
```

profile of v0, /device:TPU:1, one launch (start us, length us, event | category | flops | bytes accessed | tf_op | source)
XLA Modules:
  0.0 311.5 jit_solution(16279236654294194279)
XLA Ops:
  7.2 0.8 broadcast_multiply_fusion
  7.9 0.8 copy.22
  8.7 0.1 eq.29
  8.9 0.1 eq.25
  9.0 0.8 copy.25
  9.8 0.1 reshape.208
  10.1 0.1 mul.64
  10.2 0.6 reduce-window.6
  10.8 0.2 slice_reduce_fusion
  11.1 2.2 scatter_custom_fusion
  13.3 0.7 all_to_all.20
  14.0 10.0 %all-to-all-start = ((bf16[16,1,24]{2,1,0:T(2,128)(2,1)}), bf16[16,1,24]{2,1,0:T(2,128)(2,1)S(1)}, u32[]{:S(2)}, u32[]{:S(2)}) async-start(bf16[16,1,24]{2,1,0:T(2,128)(2,1)} %all_to_all.20), calls=%async_computation | async-start | bytes 16384 | tf_op jit(solution)/shard_map/all_to_all | solution.py:37
  24.0 10.4 %scatter_custom_fusion.1 = bf16[384,3584]{1,0:T(8,128)(2,1)} fusion(s32[256]{0:T(256)S(1)} %bitcast.59, bf16[128,3584]{1,0:T(8,128)(2,1)S(1)} %copy-done, s32[1024]{0:T(1024)S(1)} %pad_clamp_fusion.1, bf16[]{:T(256)} %constant.17.clone.1), kind=kCustom, calls=%fused_computation.21 | custom fusion | bytes 2752514 | tf_op jit(solution)/shard_map/scatter | solution.py:24
  34.4 7.2 %all-to-all-start.1 = ((bf16[16,24,3584]{2,1,0:T(8,128)(2,1)}), bf16[16,24,3584]{2,1,0:T(8,128)(2,1)}, u32[]{:S(2)}, u32[]{:S(2)}) async-start(bf16[16,24,3584]{2,1,0:T(8,128)(2,1)} %bitcast.55), calls=%async_computation.1 | async-start | bytes 5505024 | tf_op jit(solution)/shard_map/all_to_all | solution.py:30
  41.8 62.5 %all-to-all-done.1 = bf16[16,24,3584]{2,1,0:T(8,128)(2,1)} async-done(((bf16[16,24,3584]{2,1,0:T(8,128)(2,1)}), bf16[16,24,3584]{2,1,0:T(8,128)(2,1)}, u32[]{:S(2)}, u32[]{:S(2)}) %all-to-all-start.1) | async-done | bytes 2752544 | tf_op jit(solution)/shard_map/all_to_all | solution.py:30
  104.3 2.6 fusion.8
  106.9 8.9 %bitcast_reduce_fusion = (bf16[32,3584]{1,0:T(8,128)(2,1)}, f32[1024,3584]{1,0:T(8,128)}) fusion(bf16[384,3584]{1,0:T(8,128)(2,1)S(1)} %fusion.8, bf16[384,2048]{1,0:T(8,128)(2,1)S(1)} %bitcast.63), kind=kOutput, calls=%fused_computation.6 | convolution fusion | flops 2832613376 | bytes 19234816 | tf_op jit(solution)/shard_map/dot_general | solution.py:67
  115.9 91.8 %all-reduce.2.cloned.1.call-done = bf16[32,3584]{1,0:T(8,128)(2,1)} async-done(((bf16[32,3584]{1,0:T(8,128)(2,1)}), bf16[32,3584]{1,0:T(8,128)(2,1)}) %all-reduce.2.cloned.1.call-update) | async-done | bytes 229392 | tf_op jit(solution)/shard_map/pmax | solution.py:71
  207.7 1.0 convert_add_fusion
  208.7 8.4 %fusion = bf16[1024,3584]{1,0:T(8,128)(2,1)} fusion(f32[1024,3584]{1,0:T(8,128)} %get-tuple-element.19, f32[32,3584]{1,0:T(8,128)S(1)} %convert_add_fusion), kind=kLoop, calls=%fused_computation.5 | loop fusion | flops 7340032 | bytes 22478848 | tf_op jit(solution)/shard_map/convert_element_type | solution.py:73
  217.1 7.1 %fusion.11 = f32[384]{0:T(512)S(1)} fusion(bf16[1,1024,3584]{2,1,0:T(8,128)(2,1)} %param.9, bf16[384,2048]{1,0:T(8,128)(2,1)S(1)} %bitcast.64, bf16[384,3584]{1,0:T(8,128)(2,1)} %bitcast.47), kind=kOutput, calls=%fused_computation.23 | convolution fusion | flops 2825846272 | bytes 11666944 | tf_op jit(solution)/shard_map/dot_general | solution.py:54
  224.2 0.7 all_to_all.18
  224.9 9.6 %all-to-all-start.2 = ((f32[16,1,24]{2,1,0:T(1,128)}), f32[16,1,24]{2,1,0:T(1,128)S(1)}, u32[]{:S(2)}, u32[]{:S(2)}) async-start(f32[16,1,24]{2,1,0:T(1,128)} %all_to_all.18), calls=%async_computation.3 | async-start | bytes 16384 | tf_op jit(solution)/shard_map/all_to_all | solution.py:62
  234.4 2.6 multiply_convert_fusion
  237.1 6.6 %fusion.26 = (bf16[1,384,1024]{2,1,0:T(8,128)(2,1)S(1)}, bf16[1,384,1024]{2,1,0:T(8,128)(2,1)S(1)}) fusion(bf16[384,2048]{1,0:T(8,128)(2,1)S(1)} %bitcast.65, bf16[384,3584]{1,0:T(8,128)(2,1)S(1)} %bitcast.56, bf16[1,1024,3584]{2,1,0:T(8,128)(2,1)} %param.9), kind=kOutput, calls=%fused_computation.37 | convolution fusion | flops 2824470528 | bytes 13238272 | tf_op jit(solution)/shard_map/dot_general | solution.py:56
  243.7 1.3 pad_maximum_fusion
  244.9 0.5 broadcast.153
  245.5 0.7 reduce.9
  246.2 2.0 gather_fusion
  248.3 0.6 copy.27
  249.0 0.6 dynamic-slice_bitcast_fusion
  249.6 55.1 %reduce-scatter.2.cloned.1.call-done = bf16[64,3584]{1,0:T(8,128)(2,1)} async-done(((bf16[1024,3584]{1,0:T(8,128)(2,1)}), bf16[64,3584]{1,0:T(8,128)(2,1)}) %reduce-scatter.2.cloned.1.call-update) | async-done | bytes 458768 | tf_op jit(solution)/shard_map/reduce_scatter | solution.py:74
  (24 shorter events, 0.8 us)
Async XLA Ops:
  7.2 16.9 %copy-start = (bf16[128,3584]{1,0:T(8,128)(2,1)S(1)}, bf16[128,3584]{1,0:T(8,128)(2,1)}, u32[]{:S(2)}) copy-start(bf16[128,3584]{1,0:T(8,128)(2,1)} %param.5) | copy-start | bytes 2752516
  14.0 20.4 %all-to-all-start = ((bf16[16,1,24]{2,1,0:T(2,128)(2,1)}), bf16[16,1,24]{2,1,0:T(2,128)(2,1)S(1)}, u32[]{:S(2)}, u32[]{:S(2)}) async-start(bf16[16,1,24]{2,1,0:T(2,128)(2,1)} %all_to_all.20), calls=%async_computation | async-start | bytes 16384 | tf_op jit(solution)/shard_map/all_to_all | solution.py:37
  34.4 69.9 %all-to-all-start.1 = ((bf16[16,24,3584]{2,1,0:T(8,128)(2,1)}), bf16[16,24,3584]{2,1,0:T(8,128)(2,1)}, u32[]{:S(2)}, u32[]{:S(2)}) async-start(bf16[16,24,3584]{2,1,0:T(8,128)(2,1)} %bitcast.55), calls=%async_computation.1 | async-start | bytes 5505024 | tf_op jit(solution)/shard_map/all_to_all | solution.py:30
  41.7 166.1 %all-reduce.2.cloned.1.call-start = ((), (), s32[]{:S(2)}) async-start(), calls=%async_computation.4 | async-start | bytes 458752 | tf_op jit(solution)/shard_map/pmax | solution.py:71
  41.8 65.1 %copy-start.1 = (bf16[1,384,2048]{2,1,0:T(8,128)(2,1)S(1)}, bf16[1,384,2048]{2,1,0:T(8,128)(2,1)}, u32[]{:S(2)}) copy-start(bf16[1,384,2048]{2,1,0:T(8,128)(2,1)} %param.8) | copy-start | bytes 4718596
  115.8 188.8 %reduce-scatter.2.cloned.1.call-start = ((), (), s32[]{:S(2)}) async-start(), calls=%async_computation.5 | async-start | bytes 7798784 | tf_op jit(solution)/shard_map/reduce_scatter | solution.py:74
  224.9 20.0 %all-to-all-start.2 = ((f32[16,1,24]{2,1,0:T(1,128)}), f32[16,1,24]{2,1,0:T(1,128)S(1)}, u32[]{:S(2)}, u32[]{:S(2)}) async-start(f32[16,1,24]{2,1,0:T(1,128)} %all_to_all.18), calls=%async_computation.3 | async-start | bytes 16384 | tf_op jit(solution)/shard_map/all_to_all | solution.py:62
Sparse Core Ops, SparseCore 0:
  116.0 91.7 all-reduce.1
  217.2 87.4 reduce-scatter.1
where the time goes:
time: 312 us
  waiting for transfers between devices  209 us (67%)
  starting transfers between devices  26.8 us (9%)
  matrix products  22.6 us (7%)
  local copies, waits for them, and re-layouts  20.4 us (7%)
  other arithmetic  18 us (6%)
  between operations  14.2 us (5%)
    pmax x1, waiting for transfers between devices, shards(): lax.pmax(block_max.astype(jnp.bfloat16), 'dp').astype(block_max.dtype)  91.8 us
    all_to_all x1, waiting for transfers between devices, shards(): lax.all_to_all(send_rows.reshape(experts, capacity, model_width), 'expert...  62.5 us
    reduce_scatter x1, waiting for transfers between devices, shards(): lax.psum_scatter(scaled_terms, 'dp', scatter_dimension=0, tiled=True)  55.1 us
    scatter x1, local copies, waits for them, and re-layouts, shards(): jnp.zeros((slot_count, model_width), jnp.bfloat16).at[slot_index]  10.4 us
    all_to_all x1, starting transfers between devices, shards(): lax.all_to_all(send_weights.reshape(experts, capacity), 'expert', split_a...  9.98 us
    all_to_all x1, starting transfers between devices, shards(): lax.all_to_all(route_part.reshape(experts, capacity), 'expert', split_axi...  9.55 us
    dot_general x1, matrix products, shards(): lax.dot_general(hidden_act, weighted, (((0,), (0,)), ((), ())), preferred...  8.89 us
    convert_element_type x1, other arithmetic, shards(): (partial_value / jnp.repeat(scales, 32, axis=0)).astype(jnp.bfloat16)  8.35 us
  transfers between devices with their start and end apart: 5, of which 3 were waited for; matrix products, arithmetic and copies ran while one was open for 10% of the time, Pallas kernels for 0%

commit v1 on v0

v1 whole, which is shorter than its diff:
```python
import functools

import jax
import jax.numpy as jnp
from jax import lax
from jax.experimental import pallas as pl
from jax.experimental.pallas import tpu as pltpu
from jax.sharding import PartitionSpec as P

MESH = pl.DeviceIdType.MESH
F32, BF16 = jnp.float32, jnp.bfloat16
TINY = 1e-06
COLS = 256
AHEAD = 4
LAG1, LAG2 = 2, 2
Z, SIDE = 8, 4


def kernel(
    ids_ref, gate_ref, og_hbm, saved_hbm, w_hbm,
    ggu_hbm, gw_ref, ws_ref, gr_ref,
    og, saved, wmat, smat, rank_s, zsend, zrecv, wsend, wrecv, wrep, hid, hid_t,
    gact, racc, part, s1r, s2s, s2m, s2r, s2mr, rsend, rrecv, ggu,
    in_sem, w_sem, zs_sem, zr_sem, ws_sem, wr_sem, s1s_sem, s1r_sem,
    s2s_sem, s2r_sem, m2s_sem, m2r_sem, rs_sem, rr_sem, out_sem,
):
    chunks = zrecv.shape[0]
    experts, cap = zrecv.shape[1], zrecv.shape[2]
    slots, hidden = hid.shape
    dp, me = lax.axis_index("dp"), lax.axis_index("expert")
    y, x = dp // SIDE, lax.rem(dp, SIDE)
    z, core = me // 2, lax.rem(me, 2)
    quarter = hidden // SIDE
    share = quarter // SIDE

    zpeers = []
    for dz in (4, 3, 5, 2, 6, 1, 7, 0):
        for dc in (0, 1):
            if dz or dc:
                zpeers.append(lax.rem(z + dz, Z) * 2 + lax.rem(core + dc, 2))

    def along(axis, step):
        return lax.rem(y + step * (1 - axis), SIDE) * SIDE + lax.rem(x + step * axis, SIDE)

    def place(axis):
        return y * (1 - axis) + x * axis

    load_og = pltpu.make_async_copy(og_hbm, og, in_sem.at[0])
    load_saved = pltpu.make_async_copy(saved_hbm.at[0], saved, in_sem.at[1])

    def load_w(c):
        cols = pl.ds(pl.multiple_of(c * COLS, COLS), COLS)
        return pltpu.make_async_copy(w_hbm.at[0, :, cols], wmat.at[c], w_sem.at[c])

    load_og.start()
    load_saved.start()

    barrier = pltpu.get_barrier_semaphore()
    for e in zpeers:
        pl.semaphore_signal(barrier, inc=1, device_id=(dp, e), device_id_type=MESH)
    for step in (1, 2, 3):
        for axis in (0, 1):
            pl.semaphore_signal(barrier, inc=1, device_id=(along(axis, step), me), device_id_type=MESH)

    ids = ids_ref[...]
    tokens = ids.shape[1]
    gates = gate_ref[...].astype(F32)
    e_iota = lax.broadcasted_iota(jnp.int32, (experts, tokens), 0)
    first = (ids[0:1] == e_iota).astype(F32)
    second = (ids[1:2] == e_iota).astype(F32)
    named = first + second
    gate_of = first * gates[0:1] + second * gates[1:2]
    earlier = (
        lax.broadcasted_iota(jnp.int32, (tokens, tokens), 0)
        < lax.broadcasted_iota(jnp.int32, (tokens, tokens), 1)
    ).astype(F32).astype(BF16)
    rank = jnp.dot(named.astype(BF16), earlier, preferred_element_type=F32)
    rank = jnp.where(named > 0.5, rank, -1.0)
    rank_s[...] = rank
    c_iota = lax.broadcasted_iota(jnp.int32, (cap, tokens), 0).astype(F32)
    rows = []
    for e in range(experts):
        pick = jnp.where(rank[e:e + 1] == c_iota, 1.0, 0.0)
        rows.append(pick)
        gate_row = jnp.sum(pick * gate_of[e:e + 1], axis=1, keepdims=True)
        wsend[e] = jnp.broadcast_to(gate_row, (cap, 128)).astype(BF16)
    smat[...] = jnp.concatenate(rows, axis=0).astype(BF16)
    wrecv[me] = wsend[me]

    pl.semaphore_wait(barrier, len(zpeers) + 6)
    for e in zpeers:
        pltpu.make_async_remote_copy(
            src_ref=wsend.at[e], dst_ref=wrecv.at[me], send_sem=ws_sem, recv_sem=wr_sem,
            device_id=(dp, e), device_id_type=MESH,
        ).start()
    load_og.wait()

    def produce(c):
        cols = pl.ds(pl.multiple_of(c * COLS, COLS), COLS)
        block = jnp.dot(smat[...], og[:, cols], preferred_element_type=F32)
        zsend[c] = block.reshape(experts, cap, COLS).astype(BF16)
        zrecv[c, me] = zsend[c, me]
        for e in zpeers:
            pltpu.make_async_remote_copy(
                src_ref=zsend.at[c, e], dst_ref=zrecv.at[c, me],
                send_sem=zs_sem.at[c], recv_sem=zr_sem.at[c],
                device_id=(dp, e), device_id_type=MESH,
            ).start()
        load_w(c).start()

    lax.fori_loop(0, AHEAD, lambda c, _: (produce(c), 0)[1], 0)

    load_saved.wait()
    slab = 128

    def activate(i, _):
        at = pl.ds(pl.multiple_of(i * slab, slab), slab)
        gate = saved[at, :hidden].astype(F32)
        up = saved[at, hidden:].astype(F32)
        act = gate * jax.nn.sigmoid(gate) * up
        hid[at, :] = act.astype(BF16)
        hid_t[0, :, at] = act.T.astype(BF16)
        return 0

    lax.fori_loop(0, slots // slab, activate, 0)
    for a in range(SIDE):
        for b in range(SIDE):
            hid_t[1, pl.ds((b * SIDE + a) * share, share), :] = hid_t[0, pl.ds((a * SIDE + b) * share, share), :]
    gact[...] = jnp.zeros_like(gact)
    racc[...] = jnp.zeros_like(racc)

    def all_of(ref, sem):
        return pltpu.make_async_copy(ref, ref, sem)

    all_of(wrecv.at[pl.ds(0, experts - 1)], wr_sem).wait()
    wrep[...] = wrecv[...].astype(F32).reshape(slots, 128)

    def work(c):
        axis = lax.rem(c, 2)
        all_of(zrecv.at[c, pl.ds(0, experts - 1)], zr_sem.at[c]).wait()
        load_w(c).wait()
        rows = zrecv[c].astype(F32).reshape(slots, COLS)
        weight = wrep[...]
        weighted = (rows * jnp.concatenate([weight] * (COLS // 128), axis=1)).astype(BF16)
        for k in (1, 2, 3, 0):
            q = lax.rem(place(axis) + k, SIDE)
            lhs = hid_t[axis, pl.ds(pl.multiple_of(q * quarter, quarter), quarter), :]
            part[c, q] = jnp.dot(lhs, weighted, preferred_element_type=F32).astype(BF16)
            if k:
                pltpu.make_async_remote_copy(
                    src_ref=part.at[c, q], dst_ref=s1r.at[c, k - 1],
                    send_sem=s1s_sem.at[c], recv_sem=s1r_sem.at[c],
                    device_id=(along(axis, k), me), device_id_type=MESH,
                ).start()
        wc = wmat[c]
        out = jnp.dot(hid[...], wc, preferred_element_type=F32) * rows
        total = racc[...]
        for i in range(COLS // 128):
            total = total + out[:, i * 128:(i + 1) * 128]
        racc[...] = total
        gact[...] += lax.dot_general(weighted, wc, (((1,), (1,)), ((), ())), preferred_element_type=F32)

    def sum_first(c):
        axis = lax.rem(c, 2)
        mine, other = place(axis), place(1 - axis)
        all_of(s1r.at[c], s1r_sem.at[c]).wait()
        for k in (1, 2, 3, 0):
            q = lax.rem(other + k, SIDE)
            at = pl.ds(pl.multiple_of(q * share, share), share)
            total = part[c, mine, at, :].astype(F32)
            top = jnp.abs(total)
            for i in range(SIDE - 1):
                term = s1r[c, i, at, :].astype(F32)
                total = total + term
                top = jnp.maximum(top, jnp.abs(term))
            s2s[c, q] = total.astype(BF16)
            s2m[c, q] = jnp.max(top.reshape(share // 32, 32, COLS), axis=1)
            if k:
                peer = (along(1 - axis, k), me)
                pltpu.make_async_remote_copy(
                    src_ref=s2s.at[c, q], dst_ref=s2r.at[c, k - 1],
                    send_sem=s2s_sem.at[c], recv_sem=s2r_sem.at[c],
                    device_id=peer, device_id_type=MESH,
                ).start()
                pltpu.make_async_remote_copy(
                    src_ref=s2m.at[c, q], dst_ref=s2mr.at[c, k - 1],
                    send_sem=m2s_sem.at[c], recv_sem=m2r_sem.at[c],
                    device_id=peer, device_id_type=MESH,
                ).start()

    def sum_second(c):
        axis = lax.rem(c, 2)
        other = place(1 - axis)
        cols = pl.ds(pl.multiple_of(c * COLS, COLS), COLS)
        all_of(s2r.at[c], s2r_sem.at[c]).wait()
        all_of(s2mr.at[c], m2r_sem.at[c]).wait()
        total = s2s[c, other].astype(F32)
        top = s2m[c, other]
        for i in range(SIDE - 1):
            total = total + s2r[c, i].astype(F32)
            top = jnp.maximum(top, s2mr[c, i])
        scale = top + TINY
        ws_ref[0, :, cols] = scale
        parts = []
        for b in range(share // 32):
            parts.append(total[b * 32:(b + 1) * 32] / scale[b:b + 1])
        gw_ref[0, :, cols] = jnp.concatenate(parts, axis=0).astype(BF16)

    def step(c, _):
        @pl.when(c + AHEAD < chunks)
        def _():
            produce(c + AHEAD)

        work(c)

        @pl.when(c >= LAG1)
        def _():
            sum_first(c - LAG1)

        @pl.when(c >= LAG1 + LAG2)
        def _():
            sum_second(c - LAG1 - LAG2)

        return 0

    lax.fori_loop(0, chunks, step, 0)

    route = jnp.broadcast_to(jnp.sum(racc[...], axis=1, keepdims=True), (slots, 128))
    rsend[...] = route.reshape(experts, cap, 128)
    rrecv[me] = rsend[me]
    for e in zpeers:
        pltpu.make_async_remote_copy(
            src_ref=rsend.at[e], dst_ref=rrecv.at[me], send_sem=rs_sem, recv_sem=rr_sem,
            device_id=(dp, e), device_id_type=MESH,
        ).start()

    def finish(i, _):
        at = pl.ds(pl.multiple_of(i * slab, slab), slab)
        gate = saved[at, :hidden].astype(F32)
        up = saved[at, hidden:].astype(F32)
        sg = jax.nn.sigmoid(gate)
        ga = gact[at, :]
        ggu[at, :hidden] = (ga * up * sg * (1.0 + gate * (1.0 - sg))).astype(BF16)
        ggu[at, hidden:] = (ga * gate * sg).astype(BF16)
        return 0

    lax.fori_loop(0, slots // slab, finish, 0)
    store_ggu = pltpu.make_async_copy(ggu, ggu_hbm.at[0], out_sem)
    store_ggu.start()

    lax.fori_loop(chunks - LAG1, chunks, lambda c, _: (sum_first(c), 0)[1], 0)

    all_of(rrecv.at[pl.ds(0, experts - 1)], rr_sem).wait()
    ids = ids_ref[...]
    rank = rank_s[...]
    e_iota = lax.broadcasted_iota(jnp.int32, (experts, tokens), 0)
    c_iota = lax.broadcasted_iota(jnp.int32, (cap, tokens), 0).astype(F32)
    got = []
    for e in range(experts):
        got.append(jnp.sum(jnp.where(rank[e:e + 1] == c_iota, rrecv[e], 0.0), axis=0, keepdims=True))
    got = jnp.concatenate(got, axis=0)
    for k in range(2):
        gr_ref[k:k + 1, :] = jnp.sum(jnp.where(ids[k:k + 1] == e_iota, got, 0.0), axis=0, keepdims=True)

    lax.fori_loop(chunks - LAG1 - LAG2, chunks, lambda c, _: (sum_second(c), 0)[1], 0)

    store_ggu.wait()
    all_of(wsend.at[pl.ds(0, experts - 1)], ws_sem).wait()
    all_of(rsend.at[pl.ds(0, experts - 1)], rs_sem).wait()

    def drain(c, _):
        all_of(zsend.at[c, pl.ds(0, experts - 1)], zs_sem.at[c]).wait()
        all_of(s1r.at[c], s1s_sem.at[c]).wait()
        all_of(s2r.at[c], s2s_sem.at[c]).wait()
        all_of(s2mr.at[c], m2s_sem.at[c]).wait()
        return 0

    lax.fori_loop(0, chunks, drain, 0)


def shards(out_grad, route_ids, route_weights, saved_gate_up, down_weight):
    tokens, width = out_grad.shape
    hidden = down_weight.shape[1]
    experts = lax.axis_size("expert")
    slots = saved_gate_up.shape[1]
    cap = slots // experts
    chunks = width // COLS
    quarter, share = hidden // SIDE, hidden // SIDE // SIDE
    hbm, vmem = pl.BlockSpec(memory_space=pl.ANY), pl.BlockSpec(memory_space=pltpu.VMEM)
    dma = pltpu.SemaphoreType.DMA
    ggu, gw, ws, gr = pl.pallas_call(
        kernel,
        out_shape=(
            jax.ShapeDtypeStruct((1, slots, 2 * hidden), BF16),
            jax.ShapeDtypeStruct((1, share, width), BF16),
            jax.ShapeDtypeStruct((1, share // 32, width), F32),
            jax.ShapeDtypeStruct((2, tokens), F32),
        ),
        in_specs=[vmem, vmem, hbm, hbm, hbm],
        out_specs=(hbm, vmem, vmem, vmem),
        scratch_shapes=[
            pltpu.VMEM((tokens, width), BF16),
            pltpu.VMEM((slots, 2 * hidden), BF16),
            pltpu.VMEM((chunks, hidden, COLS), BF16),
            pltpu.VMEM((slots, tokens), BF16),
            pltpu.VMEM((experts, tokens), F32),
            pltpu.VMEM((chunks, experts, cap, COLS), BF16),
            pltpu.VMEM((chunks, experts, cap, COLS), BF16),
            pltpu.VMEM((experts, cap, 128), BF16),
            pltpu.VMEM((experts, cap, 128), BF16),
            pltpu.VMEM((slots, 128), F32),
            pltpu.VMEM((slots, hidden), BF16),
            pltpu.VMEM((2, hidden, slots), BF16),
            pltpu.VMEM((slots, hidden), F32),
            pltpu.VMEM((slots, 128), F32),
            pltpu.VMEM((chunks, SIDE, quarter, COLS), BF16),
            pltpu.VMEM((chunks, SIDE - 1, quarter, COLS), BF16),
            pltpu.VMEM((chunks, SIDE, share, COLS), BF16),
            pltpu.VMEM((chunks, SIDE, share // 32, COLS), F32),
            pltpu.VMEM((chunks, SIDE - 1, share, COLS), BF16),
            pltpu.VMEM((chunks, SIDE - 1, share // 32, COLS), F32),
            pltpu.VMEM((experts, cap, 128), F32),
            pltpu.VMEM((experts, cap, 128), F32),
            pltpu.VMEM((slots, 2 * hidden), BF16),
            dma((2,)), dma((chunks,)), dma((chunks,)), dma((chunks,)), dma, dma, dma((chunks,)), dma((chunks,)),
            dma((chunks,)), dma((chunks,)), dma((chunks,)), dma((chunks,)), dma, dma, dma,
        ],
        compiler_params=pltpu.CompilerParams(
            collective_id=0, has_side_effects=True, vmem_limit_bytes=60 * 2**20
        ),
    )(route_ids.T, route_weights.T, out_grad, saved_gate_up, down_weight)
    return ggu, gw, ws, gr.T


def solution(mesh):
    in_specs = (
        P(("dp", "expert"), None),
        P(("dp", "expert"), None),
        P(("dp", "expert"), None),
        P(("dp", "expert"), None, None),
        P("expert", None, None),
    )
    out_specs = (
        P(("dp", "expert"), None, None),
        P("expert", "dp", None),
        P("expert", "dp", None),
        P(("dp", "expert"), None),
    )
    return jax.shard_map(shards, mesh=mesh, in_specs=in_specs, out_specs=out_specs, check_vma=False)
```

time: 312 us -> 94.1 us (0.30)
  waiting for transfers between devices: 209 us -> 0 us
  Pallas kernels: 0 us -> 88.6 us
  starting transfers between devices: 26.8 us -> 0 us
  matrix products: 22.6 us -> 0 us
  other arithmetic: 18 us -> 0 us
  local copies, waits for them, and re-layouts: 20.4 us -> 4.73 us
  between operations: 14.2 us -> 0.67 us
    pmax x1 -> x0, waiting for transfers between devices: 91.8 us -> none  [shards(): lax.pmax(block_max.astype(jnp.bfloat16), 'dp').astype(block_max.dtype)]
    pallas_call x0 -> x1, Pallas kernels: none -> 88.6 us  [shards(): pl.pallas_call(kernel, out_shape=(jax.ShapeDtypeStruct((1, slots, 2 * hid...]
    all_to_all x3 -> x0, waiting for transfers between devices: 62.5 us -> none  [the longest x1 62.5 us: shards(): lax.all_to_all(send_rows.reshape(experts, capacity, model_width), 'expert...]
    reduce_scatter x1 -> x0, waiting for transfers between devices: 55.1 us -> none  [shards(): lax.psum_scatter(scaled_terms, 'dp', scatter_dimension=0, tiled=True)]
    all_to_all x3 -> x0, starting transfers between devices: 26.8 us -> none  [the longest x1 9.98 us: shards(): lax.all_to_all(send_weights.reshape(experts, capacity), 'expert', split_a...]
    dot_general x3 -> x0, matrix products: 22.6 us -> none  [the longest x1 8.89 us: shards(): lax.dot_general(hidden_act, weighted, (((0,), (0,)), ((), ())), preferred...]
    convert_element_type x6 -> x0, other arithmetic: 13.6 us -> none  [the longest x1 8.35 us: shards(): (partial_value / jnp.repeat(scales, 32, axis=0)).astype(jnp.bfloat16)]
    scatter x2 -> x0, local copies, waits for them, and re-layouts: 12.6 us -> none  [the longest x1 10.4 us: shards(): jnp.zeros((slot_count, model_width), jnp.bfloat16).at[slot_index]]
  transfers between devices with their start and end apart: 5 -> 0, of which waited for: 3 -> 0; matrix products, arithmetic and copies ran while one was open for 10% -> 0% of each run, Pallas kernels for 0% -> 0%
where the time goes in v1:
time: 94.1 us; the launch traced here: 94 us
  Pallas kernels  88.6 us (94%)
  local copies, waits for them, and re-layouts  4.73 us (5%)
    pallas_call x1, Pallas kernels, shards(): pl.pallas_call(kernel, out_shape=(jax.ShapeDtypeStruct((1, slots, 2 * hid...  88.6 us
    unnamed x10, local copies, waits for them, and re-layouts  4.73 us

profile of v1, /device:TPU:1, one launch (start us, length us, event | category | flops | bytes accessed | tf_op | source)
XLA Modules:
  0.0 94.0 jit_solution(16476603617652306942)
XLA Ops:
  0.6 88.6 %shard_map.84 = (bf16[1,384,2048]{2,1,0:T(8,128)(2,1)}, bf16[1,64,3584]{2,1,0:T(8,128)(2,1)}, f32[1,2,3584]{2,1,0:T(2,128)}, f32[2,128]{1,0:T(2,128)}) custom-call(s32[2,128]{1,0:T(2,128)} %bitcast.4, bf16[2,128]{1,0:T(2,128)(2,1)} %bitcast.5, bf16[128,3584]{1,0:T(8,128)(2,1)} %og_hbm.1, bf16[1,384,2048]{2,1,0:T(8,128)(2,1)} %saved_hbm.1, ...), custom_call_target="tpu_custom_call" | custom-call | tf_op jit(solution)/shard_map/pallas_call | solution.py:291
  89.2 0.0 copy-start
  89.3 0.0 copy-start.1
  89.3 0.0 copy-start.2
  89.3 2.8 %copy.13 = bf16[1,384,2048]{2,1,0:T(8,128)(2,1)} copy(bf16[1,384,2048]{2,1,0:T(8,128)(2,1)} %get-tuple-element.16) | data formatting | bytes 3145728
  92.1 0.0 copy-done
  92.1 0.8 copy.14
  92.8 0.0 copy-done.1
  92.8 0.6 copy.15
  93.4 0.0 copy-done.2
  93.4 0.6 copy.16
Async XLA Ops:
  89.2 2.8 %copy-start = (bf16[1,64,3584]{2,1,0:T(8,128)(2,1)S(1)}, bf16[1,64,3584]{2,1,0:T(8,128)(2,1)}, u32[]{:S(2)}) copy-start(bf16[1,64,3584]{2,1,0:T(8,128)(2,1)} %get-tuple-element.17) | copy-start | bytes 1376260
  89.3 3.6 %copy-start.1 = (f32[1,2,3584]{2,1,0:T(2,128)S(1)}, f32[1,2,3584]{2,1,0:T(2,128)}, u32[]{:S(2)}) copy-start(f32[1,2,3584]{2,1,0:T(2,128)} %get-tuple-element.18) | copy-start | bytes 86020
  89.3 4.2 %copy-start.2 = (f32[2,128]{1,0:T(2,128)S(1)}, f32[2,128]{1,0:T(2,128)}, u32[]{:S(2)}) copy-start(f32[2,128]{1,0:T(2,128)} %get-tuple-element.11) | copy-start | bytes 3076

commit v2 on v1

v2 whole, which is shorter than its diff:
```python
import functools

import jax
import jax.numpy as jnp
from jax import lax
from jax.experimental import pallas as pl
from jax.experimental.pallas import tpu as pltpu
from jax.sharding import PartitionSpec as P

MESH = pl.DeviceIdType.MESH
F32, BF16 = jnp.float32, jnp.bfloat16
TINY = 1e-06
COLS, HALF = 256, 128
HOPS, RELAYS = 3, 3
LAG1, LAG2 = 2, 2
Z, SIDE = 8, 4


def kernel(
    ids_ref, gate_ref, og_hbm, saved_hbm, w_hbm,
    ggu, gw_ref, ws_ref, gr_ref,
    og, saved, wmat, s_own, s_side, rank_s, hop, zown, zsend, zrecv, info_s, info, wrep, hid, hid_t,
    gact, racc, part, s1r, s2s, s2m, s2r, s2mr, rsend, rrecv,
    in_sem, w_sem, hs_sem, hr_sem, zs_sem, zr_sem, is_sem, ir_sem, s1s_sem, s1r_sem,
    s2s_sem, s2r_sem, m2s_sem, m2r_sem, rs_sem, rr_sem,
):
    chunks = zrecv.shape[0]
    experts, cap = zrecv.shape[1], zrecv.shape[2]
    slots, hidden = hid.shape
    dp, me = lax.axis_index("dp"), lax.axis_index("expert")
    y, x = dp // SIDE, lax.rem(dp, SIDE)
    z, core = me // 2, lax.rem(me, 2)
    quarter = hidden // SIDE
    share = quarter // SIDE

    def expert_at(dz, other):
        return lax.rem(z + dz + Z, Z) * 2 + (1 - core if other else core)

    zpeers = [expert_at(dz, o) for dz in (1, -1, 2, -2, 3, -3, 4, 0) for o in (0, 1) if dz or o]
    near, others = (zpeers[2], zpeers[0]), zpeers[1:2] + zpeers[3:]
    fills = [
        [expert_at(0, 0), expert_at(0, 1), expert_at(d, 0), expert_at(d, 1),
         expert_at(2 * d, 0), expert_at(2 * d, 1), expert_at(3 * d, d < 0)]
        for d in (1, -1)
    ]
    remote = experts - 3

    def along(axis, step):
        return lax.rem(y + step * (1 - axis), SIDE) * SIDE + lax.rem(x + step * axis, SIDE)

    load_og = pltpu.make_async_copy(og_hbm, og, in_sem.at[0])
    load_saved = pltpu.make_async_copy(saved_hbm.at[0], saved, in_sem.at[1])

    def load_w(c):
        cols = pl.ds(pl.multiple_of(c * COLS, COLS), COLS)
        return pltpu.make_async_copy(w_hbm.at[0, :, cols], wmat.at[c], w_sem.at[c])

    load_og.start()
    load_saved.start()

    barrier = pltpu.get_barrier_semaphore()
    for e in zpeers:
        pl.semaphore_signal(barrier, inc=1, device_id=(dp, e), device_id_type=MESH)
    for step in (1, 2, 3):
        for axis in (0, 1):
            pl.semaphore_signal(barrier, inc=1, device_id=(along(axis, step), me), device_id_type=MESH)

    tokens = ids_ref.shape[1]
    earlier = (
        lax.broadcasted_iota(jnp.int32, (tokens, tokens), 0)
        < lax.broadcasted_iota(jnp.int32, (tokens, tokens), 1)
    ).astype(F32).astype(BF16)
    c_iota = lax.broadcasted_iota(jnp.int32, (cap, tokens), 0).astype(F32)
    e_iota = lax.broadcasted_iota(jnp.int32, (experts, tokens), 0).astype(F32)
    info_s[...] = jnp.zeros_like(info_s)
    info_s[0:2, :] = ids_ref[...].astype(F32)
    info_s[2:4, :] = gate_ref[...].astype(F32)
    info[me] = info_s[...]

    def ranks(named):
        rank = jnp.dot(named.astype(F32).astype(BF16), earlier, preferred_element_type=F32)
        return jnp.where(named, rank, -1.0)

    def picks(rank_row):
        return jnp.where(rank_row == c_iota, 1.0, 0.0)

    def rank_of(i, source):
        first, second = info[source, 0:1, :], info[source, 1:2, :]
        rank_s[i] = ranks((first == e_iota) | (second == e_iota))

    rank_of(2, me)
    s_own[...] = jnp.concatenate([picks(rank_s[2, pl.ds(e, 1), :]) for e in fills[0][:2]], axis=0).astype(BF16)

    pl.semaphore_wait(barrier, len(zpeers) + 6)

    def send_hop(c):
        cols = pl.ds(pl.multiple_of(c * COLS, COLS), COLS)
        for side in (0, 1):
            pltpu.make_async_remote_copy(
                src_ref=og_hbm.at[:, cols], dst_ref=hop.at[c, side],
                send_sem=hs_sem.at[c], recv_sem=hr_sem.at[c, side],
                device_id=(dp, near[1 - side]), device_id_type=MESH,
            ).start()

    def send_info(e):
        pltpu.make_async_remote_copy(
            src_ref=info_s, dst_ref=info.at[me], send_sem=is_sem, recv_sem=ir_sem.at[me],
            device_id=(dp, e), device_id_type=MESH,
        ).start()

    def wait_info(e):
        pltpu.make_async_copy(info.at[e], info.at[e], ir_sem.at[e]).wait()

    send_info(near[0])
    send_info(near[1])
    lax.fori_loop(0, HOPS + RELAYS, lambda c, _: (send_hop(c), 0)[1], 0)
    for e in others:
        send_info(e)
    for side in (0, 1):
        wait_info(near[side])
        rank_of(side, near[side])
        s_side[side] = jnp.concatenate([picks(rank_s[side, pl.ds(e, 1), :]) for e in fills[side]], axis=0).astype(BF16)
    load_og.wait()

    def send_rows(block, c, source, target):
        pltpu.make_async_remote_copy(
            src_ref=block, dst_ref=zrecv.at[c, source],
            send_sem=zs_sem.at[c], recv_sem=zr_sem.at[c],
            device_id=(dp, target), device_id_type=MESH,
        ).start()

    def relay(c):
        cols = pl.ds(pl.multiple_of(c * COLS, COLS), COLS)
        block = jnp.dot(s_own[...], og[:, cols], preferred_element_type=F32)
        block = block.reshape(2, cap, COLS).astype(BF16)
        zrecv[c, me] = block[0]
        zown[c] = block[1]
        send_rows(zown.at[c], c, me, fills[0][1])
        for side in (0, 1):
            pltpu.make_async_copy(hop.at[c, side], hop.at[c, side], hr_sem.at[c, side]).wait()
            block = jnp.dot(s_side[side], hop[c, side], preferred_element_type=F32)
            block = block.reshape(7, cap, COLS).astype(BF16)
            zrecv[c, near[side]] = block[0]
            zsend[c, side] = block
            for i in (6, 4, 5, 2, 3, 1):
                send_rows(zsend.at[c, side, i], c, near[side], fills[side][i])
        load_w(c).start()

    lax.fori_loop(0, RELAYS, lambda c, _: (relay(c), 0)[1], 0)

    load_saved.wait()
    slab = 128

    def activate(i, _):
        at = pl.ds(pl.multiple_of(i * slab, slab), slab)
        gate = saved[at, :hidden].astype(F32)
        up = saved[at, hidden:].astype(F32)
        act = gate * jax.nn.sigmoid(gate) * up
        hid[at, :] = act.astype(BF16)
        hid_t[:, at] = act.T.astype(BF16)
        return 0

    lax.fori_loop(0, slots // slab, activate, 0)
    gact[...] = jnp.zeros_like(gact)
    racc[...] = jnp.zeros_like(racc)

    def all_of(ref, sem):
        return pltpu.make_async_copy(ref, ref, sem)

    for e in others:
        wait_info(e)
    first = jnp.concatenate([info[e, 0:1, :] for e in range(experts)], axis=0)
    second = jnp.concatenate([info[e, 1:2, :] for e in range(experts)], axis=0)
    mine = me.astype(F32)
    rank = ranks((first == mine) | (second == mine))
    for e in range(experts):
        gates = jnp.where(first[e:e + 1] == mine, info[e, 2:3, :], info[e, 3:4, :])
        weight = jnp.sum(picks(rank[e:e + 1]) * gates, axis=1, keepdims=True)
        wrep[e * cap:(e + 1) * cap, :] = jnp.broadcast_to(weight, (cap, 128))

    def send_partial(c, axis, k):
        if axis == 0:
            block = part.at[c, lax.rem(y + k, SIDE), :, :, pl.ds(0, HALF)]
        else:
            block = part.at[c, :, lax.rem(x + k, SIDE), :, pl.ds(HALF, HALF)]
        pltpu.make_async_remote_copy(
            src_ref=block, dst_ref=s1r.at[c, axis, k - 1],
            send_sem=s1s_sem.at[c, axis], recv_sem=s1r_sem.at[c, axis],
            device_id=(along(axis, k), me), device_id_type=MESH,
        ).start()

    def work(c):
        all_of(zrecv.at[c, pl.ds(0, remote)], zr_sem.at[c]).wait()
        load_w(c).wait()
        rows = zrecv[c].astype(F32).reshape(slots, COLS)
        weight = wrep[...]
        weighted = (rows * jnp.concatenate([weight] * (COLS // 128), axis=1)).astype(BF16)
        for k in (1, 2, 3, 0):
            q = lax.rem(y + k, SIDE)
            lhs = hid_t[pl.ds(pl.multiple_of(q * quarter, quarter), quarter), :]
            block = jnp.dot(lhs, weighted, preferred_element_type=F32).astype(BF16)
            part[c, q] = block.reshape(SIDE, share, COLS)
            if k:
                send_partial(c, 0, k)
        for k in (1, 2, 3):
            send_partial(c, 1, k)
        wc = wmat[c]
        out = jnp.dot(hid[...], wc, preferred_element_type=F32) * rows
        total = racc[...]
        for i in range(COLS // 128):
            total = total + out[:, i * 128:(i + 1) * 128]
        racc[...] = total
        gact[...] += lax.dot_general(weighted, wc, (((1,), (1,)), ((), ())), preferred_element_type=F32)

    def sum_first(c):
        for axis in (0, 1):
            all_of(s1r.at[c, axis], s1r_sem.at[c, axis]).wait()
            for k in (1, 2, 3, 0):
                if axis == 0:
                    q = lax.rem(x + k, SIDE)
                    total = part[c, y, q, :, 0:HALF].astype(F32)
                else:
                    q = lax.rem(y + k, SIDE)
                    total = part[c, q, x, :, HALF:COLS].astype(F32)
                top = jnp.abs(total)
                for i in range(SIDE - 1):
                    term = s1r[c, axis, i, q].astype(F32)
                    total = total + term
                    top = jnp.maximum(top, jnp.abs(term))
                s2s[c, axis, q] = total.astype(BF16)
                s2m[c, axis, q] = jnp.max(top.reshape(share // 32, 32, HALF), axis=1)
                if k:
                    peer = (along(1 - axis, k), me)
                    pltpu.make_async_remote_copy(
                        src_ref=s2s.at[c, axis, q], dst_ref=s2r.at[c, axis, k - 1],
                        send_sem=s2s_sem.at[c], recv_sem=s2r_sem.at[c, axis],
                        device_id=peer, device_id_type=MESH,
                    ).start()
                    pltpu.make_async_remote_copy(
                        src_ref=s2m.at[c, axis, q], dst_ref=s2mr.at[c, axis, k - 1],
                        send_sem=m2s_sem.at[c], recv_sem=m2r_sem.at[c, axis],
                        device_id=peer, device_id_type=MESH,
                    ).start()

    def sum_second(c):
        for axis in (0, 1):
            other = y if axis else x
            cols = pl.ds(pl.multiple_of(c * COLS + axis * HALF, HALF), HALF)
            all_of(s2r.at[c, axis], s2r_sem.at[c, axis]).wait()
            all_of(s2mr.at[c, axis], m2r_sem.at[c, axis]).wait()
            total = s2s[c, axis, other].astype(F32)
            top = s2m[c, axis, other]
            for i in range(SIDE - 1):
                total = total + s2r[c, axis, i].astype(F32)
                top = jnp.maximum(top, s2mr[c, axis, i])
            scale = top + TINY
            ws_ref[0, :, cols] = scale
            parts = []
            for b in range(share // 32):
                parts.append(total[b * 32:(b + 1) * 32] / scale[b:b + 1])
            gw_ref[0, :, cols] = jnp.concatenate(parts, axis=0).astype(BF16)

    def step(c, _):
        @pl.when(c + HOPS + RELAYS < chunks)
        def _():
            send_hop(c + HOPS + RELAYS)

        @pl.when(c + RELAYS < chunks)
        def _():
            relay(c + RELAYS)

        work(c)

        @pl.when(c >= LAG1)
        def _():
            sum_first(c - LAG1)

        @pl.when(c >= LAG1 + LAG2)
        def _():
            sum_second(c - LAG1 - LAG2)

        return 0

    lax.fori_loop(0, chunks, step, 0)
    lax.fori_loop(chunks - LAG1, chunks - 1, lambda c, _: (sum_first(c), 0)[1], 0)

    diagonal = c_iota == lax.broadcasted_iota(jnp.int32, (cap, 128), 1).astype(F32)
    for e in range(experts):
        route = jnp.sum(racc[e * cap:(e + 1) * cap, :], axis=1, keepdims=True)
        row = jnp.sum(jnp.where(diagonal, route, 0.0), axis=0, keepdims=True)
        rsend[e] = jnp.broadcast_to(row, (8, 128))
    rrecv[me] = rsend[me]
    for e in zpeers:
        pltpu.make_async_remote_copy(
            src_ref=rsend.at[e], dst_ref=rrecv.at[me], send_sem=rs_sem, recv_sem=rr_sem,
            device_id=(dp, e), device_id_type=MESH,
        ).start()

    def finish(i, _):
        at = pl.ds(pl.multiple_of(i * slab, slab), slab)
        gate = saved[at, :hidden].astype(F32)
        up = saved[at, hidden:].astype(F32)
        sg = jax.nn.sigmoid(gate)
        ga = gact[at, :]
        ggu[0, at, :hidden] = (ga * up * sg * (1.0 + gate * (1.0 - sg))).astype(BF16)
        ggu[0, at, hidden:] = (ga * gate * sg).astype(BF16)
        return 0

    lax.fori_loop(0, slots // slab, finish, 0)

    sum_first(chunks - 1)

    all_of(rrecv.at[pl.ds(0, experts - 1)], rr_sem).wait()
    got = []
    for e in range(experts):
        route = jnp.sum(jnp.where(diagonal, rrecv[e, 0:1, :], 0.0), axis=1, keepdims=True)
        got.append(jnp.sum(picks(rank_s[2, e:e + 1, :]) * route, axis=0, keepdims=True))
    got = jnp.concatenate(got, axis=0)
    for k in range(2):
        gr_ref[k:k + 1, :] = jnp.sum(jnp.where(info_s[k:k + 1, :] == e_iota, got, 0.0), axis=0, keepdims=True)

    lax.fori_loop(chunks - LAG1 - LAG2, chunks, lambda c, _: (sum_second(c), 0)[1], 0)

    all_of(info.at[pl.ds(0, experts - 1)], is_sem).wait()
    all_of(rsend.at[pl.ds(0, experts - 1)], rs_sem).wait()

    def drain(c, _):
        all_of(zrecv.at[c, pl.ds(0, remote)], zs_sem.at[c]).wait()
        all_of(hop.at[c], hs_sem.at[c]).wait()
        all_of(s1r.at[c, 0], s1s_sem.at[c, 0]).wait()
        all_of(s1r.at[c, 1], s1s_sem.at[c, 1]).wait()
        all_of(s2r.at[c], s2s_sem.at[c]).wait()
        all_of(s2mr.at[c], m2s_sem.at[c]).wait()
        return 0

    lax.fori_loop(0, chunks, drain, 0)


def store(*refs):
    sems = refs[-1]
    copies = [pltpu.make_async_copy(refs[i], refs[4 + i], sems.at[i]) for i in range(4)]
    for copy in copies:
        copy.start()
    for copy in copies:
        copy.wait()


def shards(out_grad, route_ids, route_weights, saved_gate_up, down_weight):
    tokens, width = out_grad.shape
    hidden = down_weight.shape[1]
    experts = lax.axis_size("expert")
    slots = saved_gate_up.shape[1]
    cap = slots // experts
    chunks = width // COLS
    share = hidden // SIDE // SIDE
    hbm, vmem = pl.BlockSpec(memory_space=pl.ANY), pl.BlockSpec(memory_space=pltpu.VMEM)
    dma = pltpu.SemaphoreType.DMA
    ggu, gw, ws, gr = pl.pallas_call(
        kernel,
        out_shape=(
            pltpu.VMEM((1, slots, 2 * hidden), BF16),
            pltpu.VMEM((1, share, width), BF16),
            pltpu.VMEM((1, share // 32, width), F32),
            pltpu.VMEM((2, tokens), F32),
        ),
        in_specs=[vmem, vmem, hbm, hbm, hbm],
        out_specs=(vmem,) * 4,
        scratch_shapes=[
            pltpu.VMEM((tokens, width), BF16),
            pltpu.VMEM((slots, 2 * hidden), BF16),
            pltpu.VMEM((chunks, hidden, COLS), BF16),
            pltpu.VMEM((2 * cap, tokens), BF16),
            pltpu.VMEM((2, 7 * cap, tokens), BF16),
            pltpu.VMEM((3, experts, tokens), F32),
            pltpu.VMEM((chunks, 2, tokens, COLS), BF16),
            pltpu.VMEM((chunks, cap, COLS), BF16),
            pltpu.VMEM((chunks, 2, 7, cap, COLS), BF16),
            pltpu.VMEM((chunks, experts, cap, COLS), BF16),
            pltpu.VMEM((8, tokens), F32),
            pltpu.VMEM((experts, 8, tokens), F32),
            pltpu.VMEM((slots, 128), F32),
            pltpu.VMEM((slots, hidden), BF16),
            pltpu.VMEM((hidden, slots), BF16),
            pltpu.VMEM((slots, hidden), F32),
            pltpu.VMEM((slots, 128), F32),
            pltpu.VMEM((chunks, SIDE, SIDE, share, COLS), BF16),
            pltpu.VMEM((chunks, 2, SIDE - 1, SIDE, share, HALF), BF16),
            pltpu.VMEM((chunks, 2, SIDE, share, HALF), BF16),
            pltpu.VMEM((chunks, 2, SIDE, share // 32, HALF), F32),
            pltpu.VMEM((chunks, 2, SIDE - 1, share, HALF), BF16),
            pltpu.VMEM((chunks, 2, SIDE - 1, share // 32, HALF), F32),
            pltpu.VMEM((experts, 8, 128), F32),
            pltpu.VMEM((experts, 8, 128), F32),
            dma((2,)), dma((chunks,)), dma((chunks,)), dma((chunks, 2)), dma((chunks,)), dma((chunks,)), dma, dma((experts,)),
            dma((chunks, 2)), dma((chunks, 2)),
            dma((chunks,)), dma((chunks, 2)), dma((chunks,)), dma((chunks, 2)), dma, dma,
        ],
        compiler_params=pltpu.CompilerParams(
            collective_id=0, has_side_effects=True, vmem_limit_bytes=52 * 2**20
        ),
    )(route_ids.T, route_weights.T, out_grad, saved_gate_up, down_weight)
    ggu, gw, ws, gr = (pltpu.with_memory_space_constraint(o, pltpu.VMEM) for o in (ggu, gw, ws, gr))
    ggu, gw, ws, gr = pl.pallas_call(
        store,
        out_shape=tuple(jax.ShapeDtypeStruct(o.shape, o.dtype) for o in (ggu, gw, ws, gr)),
        in_specs=[vmem] * 4,
        out_specs=(hbm,) * 4,
        scratch_shapes=[dma((4,))],
        compiler_params=pltpu.CompilerParams(vmem_limit_bytes=2**20),
    )(ggu, gw, ws, gr)
    return ggu, gw, ws, gr.T


def solution(mesh):
    in_specs = (
        P(("dp", "expert"), None),
        P(("dp", "expert"), None),
        P(("dp", "expert"), None),
        P(("dp", "expert"), None, None),
        P("expert", None, None),
    )
    out_specs = (
        P(("dp", "expert"), None, None),
        P("expert", "dp", None),
        P("expert", "dp", None),
        P(("dp", "expert"), None),
    )
    return jax.shard_map(shards, mesh=mesh, in_specs=in_specs, out_specs=out_specs, check_vma=False)
```

time: 94.1 us -> 86.8 us (0.922)
  local copies, waits for them, and re-layouts: 4.73 us -> 0 us
  Pallas kernels: 88.6 us -> 86.1 us
    unnamed x10 -> x0, local copies, waits for them, and re-layouts: 4.73 us -> none
    pallas_call x1 -> x2, Pallas kernels: 88.6 us -> 86.1 us  [the longest x1 84.8 us: shards(): pl.pallas_call(kernel, out_shape=(pltpu.VMEM((1, slots, 2 * hidden), BF16...]
where the time goes in v2:
time: 86.8 us; the launch traced here: 86.7 us
  Pallas kernels  86.1 us (99%)
    pallas_call x1, Pallas kernels, shards(): pl.pallas_call(kernel, out_shape=(pltpu.VMEM((1, slots, 2 * hidden), BF16...  84.8 us

profile of v2, /device:TPU:1, one launch (start us, length us, event | category | flops | bytes accessed | tf_op | source)
XLA Modules:
  0.0 86.7 jit_solution(11480855281010220347)
XLA Ops:
  0.6 84.8 %shard_map.84 = (bf16[1,384,2048]{2,1,0:T(8,128)(2,1)S(1)}, bf16[1,64,3584]{2,1,0:T(8,128)(2,1)S(1)}, f32[1,2,3584]{2,1,0:T(2,128)S(1)}, f32[2,128]{1,0:T(2,128)S(1)}) custom-call(s32[2,128]{1,0:T(2,128)} %bitcast.3, bf16[2,128]{1,0:T(2,128)(2,1)} %bitcast.4, bf16[128,3584]{1,0:T(8,128)(2,1)} %og_hbm.1, bf16[1,384,2048]{2,1,0:T(8,128)(2,1)} %saved_hbm.1, ...), custom_call_target="tpu_custom_call" | custom-call | tf_op jit(solution)/shard_map/pallas_call | solution.py:358
  85.4 1.3 %shard_map.85 = (bf16[1,384,2048]{2,1,0:T(8,128)(2,1)}, bf16[1,64,3584]{2,1,0:T(8,128)(2,1)}, f32[1,2,3584]{2,1,0:T(2,128)}, f32[2,128]{1,0:T(2,128)}) custom-call(bf16[1,384,2048]{2,1,0:T(8,128)(2,1)S(1)} %get-tuple-element.12.refs_0_, bf16[1,64,3584]{2,1,0:T(8,128)(2,1)S(1)} %get-tuple-element.13.refs_1_, f32[1,2,3584]{2,1,0:T(2,128)S(1)} %get-tuple-element.14.refs_2_, ...), custom_call_target="tpu_custom_call" | custom-call | tf_op jit(solution)/shard_map/pallas_call | solution.py:403

commit v3 on v2

--- a/solution.py
+++ b/solution.py
@@ -11,7 +11,7 @@
 F32, BF16 = jnp.float32, jnp.bfloat16
 TINY = 1e-06
 COLS, HALF = 256, 128
-HOPS, RELAYS = 3, 3
+HOPS, RELAYS = 1, 3
 LAG1, LAG2 = 2, 2
 Z, SIDE = 8, 4
 
@@ -265,15 +265,16 @@
         def _():
             send_hop(c + HOPS + RELAYS)
 
+
+        @pl.when(c >= LAG1)
+        def _():
+            sum_first(c - LAG1)
+
+        work(c)
+
         @pl.when(c + RELAYS < chunks)
         def _():
             relay(c + RELAYS)
-
-        work(c)
-
-        @pl.when(c >= LAG1)
-        def _():
-            sum_first(c - LAG1)
 
         @pl.when(c >= LAG1 + LAG2)
         def _():

time: 86.8 us -> 84.9 us (0.978)
  Pallas kernels: 86.1 us -> 83.7 us
    pallas_call x1, Pallas kernels: 84.8 us -> 82.4 us  [shards(): pl.pallas_call(kernel, out_shape=(pltpu.VMEM((1, slots, 2 * hidden), BF16...]
where the time goes in v3:
time: 84.9 us; the launch traced here: 84.3 us
  Pallas kernels  83.7 us (99%)
    pallas_call x1, Pallas kernels, shards(): pl.pallas_call(kernel, out_shape=(pltpu.VMEM((1, slots, 2 * hidden), BF16...  82.4 us

profile of v3, /device:TPU:1, one launch (start us, length us, event | category | flops | bytes accessed | tf_op | source)
XLA Modules:
  0.0 84.3 jit_solution(7378664547859567107)
XLA Ops:
  0.6 82.4 %shard_map.84 = (bf16[1,384,2048]{2,1,0:T(8,128)(2,1)S(1)}, bf16[1,64,3584]{2,1,0:T(8,128)(2,1)S(1)}, f32[1,2,3584]{2,1,0:T(2,128)S(1)}, f32[2,128]{1,0:T(2,128)S(1)}) custom-call(s32[2,128]{1,0:T(2,128)} %bitcast.3, bf16[2,128]{1,0:T(2,128)(2,1)} %bitcast.4, bf16[128,3584]{1,0:T(8,128)(2,1)} %og_hbm.1, bf16[1,384,2048]{2,1,0:T(8,128)(2,1)} %saved_hbm.1, ...), custom_call_target="tpu_custom_call" | custom-call | tf_op jit(solution)/shard_map/pallas_call | solution.py:359
  83.0 1.3 %shard_map.85 = (bf16[1,384,2048]{2,1,0:T(8,128)(2,1)}, bf16[1,64,3584]{2,1,0:T(8,128)(2,1)}, f32[1,2,3584]{2,1,0:T(2,128)}, f32[2,128]{1,0:T(2,128)}) custom-call(bf16[1,384,2048]{2,1,0:T(8,128)(2,1)S(1)} %get-tuple-element.12.refs_0_, bf16[1,64,3584]{2,1,0:T(8,128)(2,1)S(1)} %get-tuple-element.13.refs_1_, f32[1,2,3584]{2,1,0:T(2,128)S(1)} %get-tuple-element.14.refs_2_, ...), custom_call_target="tpu_custom_call" | custom-call | tf_op jit(solution)/shard_map/pallas_call | solution.py:404

commit v4 on v3

--- a/solution.py
+++ b/solution.py
@@ -91,13 +91,14 @@
     rank_of(2, me)
     s_own[...] = jnp.concatenate([picks(rank_s[2, pl.ds(e, 1), :]) for e in fills[0][:2]], axis=0).astype(BF16)
 
+    load_og.wait()
     pl.semaphore_wait(barrier, len(zpeers) + 6)
 
     def send_hop(c):
         cols = pl.ds(pl.multiple_of(c * COLS, COLS), COLS)
         for side in (0, 1):
             pltpu.make_async_remote_copy(
-                src_ref=og_hbm.at[:, cols], dst_ref=hop.at[c, side],
+                src_ref=og.at[:, cols], dst_ref=hop.at[c, side],
                 send_sem=hs_sem.at[c], recv_sem=hr_sem.at[c, side],
                 device_id=(dp, near[1 - side]), device_id_type=MESH,
             ).start()
@@ -120,7 +121,6 @@
         wait_info(near[side])
         rank_of(side, near[side])
         s_side[side] = jnp.concatenate([picks(rank_s[side, pl.ds(e, 1), :]) for e in fills[side]], axis=0).astype(BF16)
-    load_og.wait()
 
     def send_rows(block, c, source, target):
         pltpu.make_async_remote_copy(
@@ -142,7 +142,7 @@
             block = block.reshape(7, cap, COLS).astype(BF16)
             zrecv[c, near[side]] = block[0]
             zsend[c, side] = block
-            for i in (6, 4, 5, 2, 3, 1):
+            for i in (1, 2, 3, 4, 5, 6):
                 send_rows(zsend.at[c, side, i], c, near[side], fills[side][i])
         load_w(c).start()
 

time: 84.9 us -> 84.3 us (level)
  Pallas kernels: 83.7 us -> 82.8 us
    pallas_call x1, Pallas kernels: 82.4 us -> 81.5 us  [shards(): pl.pallas_call(kernel, out_shape=(pltpu.VMEM((1, slots, 2 * hidden), BF16...]
where the time goes in v4:
time: 84.3 us; the launch traced here: 83.4 us
  Pallas kernels  82.8 us (98%)
    pallas_call x1, Pallas kernels, shards(): pl.pallas_call(kernel, out_shape=(pltpu.VMEM((1, slots, 2 * hidden), BF16...  81.5 us

profile of v4, /device:TPU:1, one launch (start us, length us, event | category | flops | bytes accessed | tf_op | source)
XLA Modules:
  0.0 83.4 jit_solution(15798196083171766805)
XLA Ops:
  0.6 81.5 %shard_map.84 = (bf16[1,384,2048]{2,1,0:T(8,128)(2,1)S(1)}, bf16[1,64,3584]{2,1,0:T(8,128)(2,1)S(1)}, f32[1,2,3584]{2,1,0:T(2,128)S(1)}, f32[2,128]{1,0:T(2,128)S(1)}) custom-call(s32[2,128]{1,0:T(2,128)} %bitcast.3, bf16[2,128]{1,0:T(2,128)(2,1)} %bitcast.4, bf16[128,3584]{1,0:T(8,128)(2,1)} %og_hbm.1, bf16[1,384,2048]{2,1,0:T(8,128)(2,1)} %saved_hbm.1, ...), custom_call_target="tpu_custom_call" | custom-call | tf_op jit(solution)/shard_map/pallas_call | solution.py:359
  82.1 1.3 %shard_map.85 = (bf16[1,384,2048]{2,1,0:T(8,128)(2,1)}, bf16[1,64,3584]{2,1,0:T(8,128)(2,1)}, f32[1,2,3584]{2,1,0:T(2,128)}, f32[2,128]{1,0:T(2,128)}) custom-call(bf16[1,384,2048]{2,1,0:T(8,128)(2,1)S(1)} %get-tuple-element.12.refs_0_, bf16[1,64,3584]{2,1,0:T(8,128)(2,1)S(1)} %get-tuple-element.13.refs_1_, f32[1,2,3584]{2,1,0:T(2,128)S(1)} %get-tuple-element.14.refs_2_, ...), custom_call_target="tpu_custom_call" | custom-call | tf_op jit(solution)/shard_map/pallas_call | solution.py:404
